TPU v7x, 512 devices: a whole 4x8x8 slice. The times are simulated.
512 devices in a mesh: hours: 64 (over z, x, core), region: 8 (over y).
Axes of the slice: x: 4, y: 8, z: 8, core: 2. Of those that a mesh axis runs over, the one named last changes fastest.
Arguments:
- availability: float32 [4096, 16, 1024], P('hours', None, 'region'), may hold values from 0.1 to 1
- demand: float32 [4096, 1024], P('hours', 'region'), may hold values from 2 to 72, as said below
- gen_cost: float32 [16, 1024], P(None, 'region'), may hold values from 0.05 to 1
- cap_cost: float32 [8, 2048], P('region', 'hours'), may hold values from 204.8 to 2048
- owner_map: int32 [8, 2048], P('region'), may hold values from 0 to 2047, each once within a row
- line_ends: int32 [2, 2048], P(None, 'region'), may hold values from 0 to 127
- line_limit: float32 [2048], P('region'), may hold values from 0.5 to 4
- cross_ends: int32 [2, 8, 256], P(None, 'region'), may hold values from 0 to 127
- cross_limit: float32 [8, 256], P('region'), may hold values from 0.5 to 4
- pair_counts: int32 [8, 8], P('region'), may hold values from 0 to 32, as said below
- store_node: int32 [2048], P('region'), may hold values from 0 to 127
- store_energy: float32 [2048], P('region'), may hold values from 0.02 to 0.4
- store_power: float32 [2048], P('region'), may hold values from 0.2 to 2
- price_start: float32 [4096, 1024], P('hours', 'region'), may hold values from -3 to 0.5
Outputs:
- dispatch: float32 [4096, 16, 1024], P('hours', None, 'region')
- capacity: float32 [8, 2048], P('region', 'hours')
- prices: float32 [4096, 1024], P('hours', 'region')
- charge_state: float32 [4096, 2048], P('hours', 'region')
Inputs may be any that keep to these rules, and one draw needn't show every extreme that they name: `demand`: loads are positive. `owner_map`: each row lists every capacity column of its region once. `pair_counts`: cross lines in use among the 32 slots of each ordered pair of regions; a region has none to itself; some pair uses all 32.
All inputs are finite; a program needn't handle non-finite values.
Results may differ from a plain program's by a relative error of at most 0.00018.
Values sent between devices are 32-bit elements; how exact they have to be, the bound alone decides.
A program may use at most 64 MiB of HBM per device.

v0:
```python
import jax
import jax.numpy as jnp
from jax import lax
from jax.sharding import PartitionSpec as P

ITERS = 4
epsilon = 1e-06
highest = lax.Precision.HIGHEST


def shifted(value, axis, steps):
    count = lax.axis_size(axis)
    pairs = [(source, (source + steps) % count) for source in range(count)]
    return lax.ppermute(value, axis, pairs)


def one_hot(indices, labels):
    return (indices[:, None] == labels[None, :]).astype(jnp.float32)


def to_owners(partial_value, owned_cols):
    summed = lax.psum(partial_value, "hours")
    return lax.dynamic_slice_in_dim(summed, lax.axis_index("hours") * owned_cols, owned_cols)


def spread_columns(capacity_bar):
    return lax.all_gather(capacity_bar, "hours", axis=0, tiled=True)


def body(
    availability,
    demand,
    gen_cost,
    cap_cost,
    owner_map,
    line_ends,
    line_limit,
    cross_ends,
    cross_limit,
    pair_counts,
    store_node,
    store_energy,
    store_power,
    price_start,
):
    hour_rows, tech_count, node_count = availability.shape
    region_count = lax.axis_size("region")
    slot_count = cross_limit.shape[1]
    slot_width = slot_count // region_count
    owned_cols = cap_cost.shape[1]
    owner_cols = owner_map[0]
    inverse = jnp.argsort(owner_cols)
    node_ids = jnp.arange(node_count, dtype=jnp.int32)
    line_inc = one_hot(line_ends[1], node_ids) - one_hot(line_ends[0], node_ids)
    store_map = one_hot(store_node, node_ids)
    leave_map = one_hot(cross_ends[0, 0], node_ids)
    slot_ids = jnp.arange(slot_count, dtype=jnp.int32)
    pair_of = slot_ids // slot_width
    region_ids = jnp.arange(region_count, dtype=jnp.int32)
    in_use = jnp.sum(
        jnp.where(pair_of[:, None] == region_ids[None, :], pair_counts[0][None, :], 0), axis=1
    )
    cross_bound = jnp.where(slot_ids % slot_width < in_use, cross_limit[0], 0.0)
    reach_map = one_hot(
        pair_of * node_count + cross_ends[1, 0],
        jnp.arange(region_count * node_count, dtype=jnp.int32),
    )
    column_costs = cap_cost[0]
    col_weight = to_owners(jnp.sum(availability, axis=0).reshape(-1)[owner_cols], owned_cols)
    dispatch = jnp.zeros_like(availability)
    capacity = jnp.zeros((owned_cols,), jnp.float32)
    inner_flow = jnp.zeros((hour_rows, line_limit.shape[0]), jnp.float32)
    cross_flow = jnp.zeros((hour_rows, slot_count), jnp.float32)
    mirror_flow = jnp.zeros((hour_rows, slot_count), jnp.float32)
    discharge = jnp.zeros((hour_rows, store_node.shape[0]), jnp.float32)
    charge = jnp.zeros((hour_rows, store_node.shape[0]), jnp.float32)
    prices = price_start
    cap_duals = jnp.zeros_like(availability)
    store_duals = jnp.zeros((hour_rows, store_node.shape[0]), jnp.float32)
    weight = jnp.float32(1.0)
    for iteration in range(ITERS):
        final_sweep = iteration == ITERS - 1
        primal_step = 0.5 / weight
        far_side = jnp.dot(
            lax.all_gather(prices, "region", axis=1, tiled=True), reach_map.T, precision=highest
        )
        if iteration == 0:
            next_duals = jnp.zeros_like(store_duals)
            cap_pull = jnp.zeros((owned_cols,), jnp.float32)
        else:
            next_row = shifted(store_duals[:1], "hours", -1)
            next_duals = jnp.concatenate([store_duals[1:], next_row], axis=0)
            cap_pull = to_owners(
                jnp.sum(availability * cap_duals, axis=0).reshape(-1)[owner_cols], owned_cols
            )
        dispatch_new = jnp.maximum(
            dispatch - primal_step * (gen_cost[None] + prices[:, None, :] + cap_duals), 0.0
        )
        capacity_new = jnp.maximum(
            capacity - (column_costs - cap_pull) / (weight * col_weight), 0.0
        )
        inner_new = jnp.clip(
            inner_flow - primal_step * jnp.dot(prices, line_inc.T, precision=highest),
            -line_limit,
            line_limit,
        )
        cross_new = jnp.clip(
            cross_flow - primal_step * (far_side - jnp.dot(prices, leave_map.T, precision=highest)),
            -cross_bound,
            cross_bound,
        )
        mirror_new = mirror_flow
        discharge_new = jnp.clip(
            discharge
            - primal_step * (jnp.dot(prices, store_map.T, precision=highest) + store_duals),
            -store_power,
            store_power,
        )
        charge_new = jnp.clip(charge - primal_step * (store_duals - next_duals), 0.0, store_energy)
        if not final_sweep:
            cap_change = capacity_new - capacity
            primal_sq = (
                jnp.sum((dispatch_new - dispatch) ** 2)
                + jnp.sum(cap_change**2)
                + jnp.sum((inner_new - inner_flow) ** 2)
                + jnp.sum((cross_new - cross_flow) ** 2)
                + jnp.sum((discharge_new - discharge) ** 2)
                + jnp.sum((charge_new - charge) ** 2)
            )
            primal_sum = lax.psum(primal_sq, ("hours", "region"))
        dispatch_bar = 2.0 * dispatch_new - dispatch
        capacity_bar = 2.0 * capacity_new - capacity
        inner_bar = 2.0 * inner_new - inner_flow
        cross_bar = 2.0 * cross_new - cross_flow
        discharge_bar = 2.0 * discharge_new - discharge
        charge_bar = 2.0 * charge_new - charge
        capacity_all = spread_columns(capacity_bar)
        cap_dense = capacity_all[inverse].reshape(tech_count, node_count)
        per_dest = jnp.dot(cross_bar, reach_map, precision=highest)
        balance = (
            jnp.sum(dispatch_bar, axis=1)
            + jnp.dot(inner_bar, line_inc, precision=highest)
            + (
                lax.psum_scatter(per_dest, "region", scatter_dimension=1, tiled=True)
                - jnp.dot(cross_bar, leave_map, precision=highest)
            )
            + jnp.dot(discharge_bar, store_map, precision=highest)
            - demand
        )
        prev_row = shifted(charge_bar[-1:], "hours", 1)
        storage_rows = (
            charge_bar - jnp.concatenate([prev_row, charge_bar[:-1]], axis=0) + discharge_bar
        )
        cap_rows = dispatch_bar - availability * cap_dense[None]
        prices_new = prices + weight / (tech_count + 8.0) * balance
        cap_new = jnp.maximum(cap_duals + weight / 2.0 * cap_rows, 0.0)
        store_new = store_duals + weight / 3.0 * storage_rows
        if not final_sweep:
            dual_sq = (
                jnp.sum((prices_new - prices) ** 2)
                + jnp.sum((cap_new - cap_duals) ** 2)
                + jnp.sum((store_new - store_duals) ** 2)
            )
            dual_sum = lax.psum(dual_sq, ("hours", "region"))
            weight = jnp.sqrt(weight * jnp.sqrt((dual_sum + epsilon) / (primal_sum + epsilon)))
        dispatch, capacity, inner_flow, cross_flow = (
            dispatch_new,
            capacity_new,
            inner_new,
            cross_new,
        )
        mirror_flow = mirror_new
        discharge, charge = (discharge_new, charge_new)
        prices, cap_duals, store_duals = (prices_new, cap_new, store_new)
    return (dispatch, capacity[None], prices, charge)


def solution(mesh):
    placed = (
        P("hours", None, "region"),
        P("hours", "region"),
        P(None, "region"),
        P("region", "hours"),
        P("region", None),
        P(None, "region"),
        P("region"),
        P(None, "region", None),
        P("region", None),
        P("region", None),
        P("region"),
        P("region"),
        P("region"),
        P("hours", "region"),
    )
    return jax.shard_map(
        body,
        mesh=mesh,
        in_specs=placed,
        out_specs=(
            P("hours", None, "region"),
            P("region", "hours"),
            P("hours", "region"),
            P("hours", "region"),
        ),
        check_vma=False,
    )
```

profile of v0, /device:TPU:2, one launch (start us, length us, event | category | flops | bytes accessed | tf_op | source)
XLA Modules:
  0.0 1496.5 jit_solution(16780039333863139814)
XLA Ops:
  7.9 2.0 collective-permute-start
  10.0 26.6 %all_gather.21 = f32[64,1024]{1,0:T(8,128)S(1)} all-gather(f32[64,128]{1,0:T(8,128)} %param.27), channel_id=1, replica_groups=mesh['hours'=64,'region'=8] {'region'}, dimensions={1}, use_global_device_ids=true | all-gather | bytes 294912 | tf_op jit(solution)/shard_map/all_gather | solution.py:85
  39.0 1.3 fusion.74
  41.2 11.8 gather_fusion
  53.0 126.8 %psum.70 = f32[2048]{0:T(1024)S(1)} all-reduce(f32[2048]{0:T(1024)S(1)} %gather_fusion), channel_id=1, replica_groups=mesh['hours'=64,'region'=8] {'hours'}, use_global_device_ids=true, to_apply=%region_5.6 | all-reduce | flops 2048 | bytes 16384 | tf_op jit(solution)/shard_map/psum | solution.py:22
  179.7 1.3 dynamic-slice
  182.5 126.4 %all-reduce = f32[2048]{0:T(1024)S(1)} all-reduce(f32[2048]{0:T(1024)S(1)} %multiply_dynamic-update-slice_fusion), channel_id=1, replica_groups=mesh['hours'=64,'region'=8] {'hours'}, use_global_device_ids=true, to_apply=%add | all-reduce | flops 2048 | bytes 16384
  308.9 5.0 sort.17
  314.0 11.8 gather_fusion.1
  325.8 1.1 multiply_reduce_fusion.6
  326.8 11.8 gather_fusion.2
  338.6 1.0 multiply_reduce_fusion.21
  340.6 126.1 %psum.73 = f32[2048]{0:T(1024)S(1)} all-reduce(f32[2048]{0:T(1024)S(1)} %gather_fusion.2), channel_id=1, replica_groups=mesh['hours'=64,'region'=8] {'hours'}, use_global_device_ids=true, to_apply=%region_21.22 | all-reduce | flops 2048 | bytes 16384 | tf_op jit(solution)/shard_map/psum | solution.py:22
  472.2 1.0 fusion.67
  476.0 7.0 collective-permute-start.1
  483.0 95.3 %all-reduce.5 = (f32[]{:T(128)}, f32[]{:T(128)}) all-reduce(f32[]{:T(128)S(6)} %add.309, f32[]{:T(128)S(6)} %add.315), channel_id=1, replica_groups=mesh['hours'=64,'region'=8] {'hours','region'}, use_global_device_ids=true, to_apply=%region_9.10 | all-reduce | flops 2 | bytes 16 | tf_op jit(solution)/shard_map/psum | solution.py:164
  579.7 24.8 %all_gather.23 = f32[64,1024]{1,0:T(8,128)S(1)} all-gather(f32[64,128]{1,0:T(8,128)S(1)} %get-tuple-element.56), channel_id=1, replica_groups=mesh['hours'=64,'region'=8] {'region'}, dimensions={1}, use_global_device_ids=true | all-gather | bytes 294912 | tf_op jit(solution)/shard_map/all_gather | solution.py:85
  604.5 1.0 multiply_reduce_fusion.17
  606.4 120.4 %all-reduce.1 = f32[2048]{0:T(1024)S(1)} all-reduce(f32[2048]{0:T(1024)S(1)} %subtract_dynamic-update-slice_fusion.1), channel_id=1, replica_groups=mesh['hours'=64,'region'=8] {'hours'}, use_global_device_ids=true, to_apply=%add.1 | all-reduce | flops 2048 | bytes 16384
  726.8 11.8 gather_fusion.3
  740.7 0.9 multiply_reduce_fusion.16
  741.6 1.3 fusion.72
  742.9 1.2 multiply_reduce_fusion.3
  744.2 11.8 gather_fusion.4
  756.0 1.9 collective-permute-start.2
  758.2 131.1 %psum.76 = f32[2048]{0:T(1024)S(1)} all-reduce(f32[2048]{0:T(1024)S(1)} %gather_fusion.4), channel_id=1, replica_groups=mesh['hours'=64,'region'=8] {'hours'}, use_global_device_ids=true, to_apply=%region_36.37 | all-reduce | flops 2048 | bytes 16384 | tf_op jit(solution)/shard_map/psum | solution.py:22
  891.9 1.0 multiply_reduce_fusion.15
  894.2 1.0 fusion.63
  898.0 1.9 collective-permute-start.3
  900.0 100.8 %all-reduce.4 = (f32[]{:T(128)}, f32[]{:T(128)}) all-reduce(f32[]{:T(128)S(6)} %add.329, f32[]{:T(128)S(6)} %add.335), channel_id=1, replica_groups=mesh['hours'=64,'region'=8] {'hours','region'}, use_global_device_ids=true, to_apply=%region_24.25 | all-reduce | flops 2 | bytes 16 | tf_op jit(solution)/shard_map/psum | solution.py:164
  1002.9 1.0 multiply_reduce_fusion.12
  1003.9 24.8 %all_gather.25 = f32[64,1024]{1,0:T(8,128)S(1)} all-gather(f32[64,128]{1,0:T(8,128)S(1)} %get-tuple-element.63), channel_id=1, replica_groups=mesh['hours'=64,'region'=8] {'region'}, dimensions={1}, use_global_device_ids=true | all-gather | bytes 294912 | tf_op jit(solution)/shard_map/all_gather | solution.py:85
  1029.5 120.4 %all-reduce.2 = f32[2048]{0:T(1024)S(1)} all-reduce(f32[2048]{0:T(1024)S(1)} %subtract_dynamic-update-slice_fusion), channel_id=1, replica_groups=mesh['hours'=64,'region'=8] {'hours'}, use_global_device_ids=true, to_apply=%add.2 | all-reduce | flops 2048 | bytes 16384
  1149.9 11.8 gather_fusion.5
  1161.7 1.9 collective-permute-start.4
  1164.4 0.9 multiply_reduce_fusion.11
  1165.3 1.3 fusion.70
  1166.7 1.4 multiply_reduce_fusion
  1168.1 11.8 gather_fusion.6
  1180.2 131.1 %psum.79 = f32[2048]{0:T(1024)S(1)} all-reduce(f32[2048]{0:T(1024)S(1)} %gather_fusion.6), channel_id=1, replica_groups=mesh['hours'=64,'region'=8] {'hours'}, use_global_device_ids=true, to_apply=%region_48.49 | all-reduce | flops 2048 | bytes 16384 | tf_op jit(solution)/shard_map/psum | solution.py:22
  1316.2 1.0 fusion.59
  1320.0 1.9 collective-permute-start.5
  1321.9 100.9 %all-reduce.3 = (f32[]{:T(128)}, f32[]{:T(128)}) all-reduce(f32[]{:T(128)S(6)} %add.349, f32[]{:T(128)S(6)} %add.355), channel_id=1, replica_groups=mesh['hours'=64,'region'=8] {'hours','region'}, use_global_device_ids=true, to_apply=%region_39.40 | all-reduce | flops 2 | bytes 16 | tf_op jit(solution)/shard_map/psum | solution.py:164
  1424.3 24.8 %all_gather.27 = f32[64,1024]{1,0:T(8,128)S(1)} all-gather(f32[64,128]{1,0:T(8,128)S(1)} %get-tuple-element.70), channel_id=1, replica_groups=mesh['hours'=64,'region'=8] {'region'}, dimensions={1}, use_global_device_ids=true | all-gather | bytes 294912 | tf_op jit(solution)/shard_map/all_gather | solution.py:85
  1449.5 1.6 subtract_reduce_fusion
  1452.1 1.3 fusion.68
  1455.2 32.9 %reduce-scatter.11.cloned.1.call-done = f32[64,128]{1,0:T(8,128)} async-done(((f32[64,1024]{1,0:T(8,128)}), f32[64,128]{1,0:T(8,128)}) %reduce-scatter.11.cloned.1.call-update) | async-done | bytes 32784 | tf_op jit(solution)/shard_map/reduce_scatter | solution.py:144
  1488.1 1.0 fusion.55
  (102 shorter events, 20.9 us)
Async XLA Ops:
  7.2 465.0 %reduce-scatter.5.cloned.1.call-start = ((), (), s32[]{:S(2)}) async-start(), calls=%async_computation.4 | async-start | bytes 294912 | tf_op jit(solution)/shard_map/reduce_scatter | solution.py:144
  7.9 2.1 copy-start.9
  7.9 461.4 %collective-permute-start = (f32[1,256]{1,0:T(1,128)S(1)}, f32[1,256]{1,0:T(1,128)S(1)}, u32[]{:S(2)}, u32[]{:S(2)}) collective-permute-start(f32[1,256]{1,0:T(1,128)S(1)} %bitcast.122), channel_id=1, source_target_pairs={{0,8},{8,16},{16,24},{24,32},{32,40},{40,48},{48,56},{56,64},{64,7... | collective-permute-start | bytes 3080 | tf_op jit(solution)/shard_map/ppermute | solution.py:14
  36.6 0.7 copy-start.13
  36.6 0.7 copy-start.12
  37.2 0.8 copy-start.1
  37.3 3.8 copy-start
  40.3 853.9 %reduce-scatter.7.cloned.1.call-start = ((), (), s32[]{:S(2)}) async-start(), calls=%async_computation.5 | async-start | bytes 294912 | tf_op jit(solution)/shard_map/reduce_scatter | solution.py:144
  40.3 0.7 copy-start.11
  40.3 0.7 copy-start.5
  40.4 0.7 copy-start.10
  181.0 0.7 copy-start.8
  314.0 11.8 copy-start.3
  340.6 126.1 %copy-start.7 = (f32[256]{0:T(256)S(1)}, f32[256]{0:T(256)}, u32[]{:S(2)}) copy-start(f32[256]{0:T(256)} %param.26) | copy-start | bytes 3076
  469.2 0.7 copy-start.4
  472.1 1.1 copy-start.2
  476.0 262.6 %collective-permute-start.1 = (f32[1,256]{1,0:T(1,128)S(1)}, f32[1,256]{1,0:T(1,128)S(1)}, u32[]{:S(2)}, u32[]{:S(2)}) collective-permute-start(f32[1,256]{1,0:T(1,128)S(1)} %slice.79), channel_id=1, source_target_pairs={{0,504},{8,0},{16,8},{24,16},{32,24},{40,32},{48,40},{56,48},{64,5... | collective-permute-start | bytes 3080 | tf_op jit(solution)/shard_map/ppermute | solution.py:14
  738.6 0.7 copy-start.6
  742.9 573.2 %reduce-scatter.9.cloned.1.call-start = ((), (), s32[]{:S(2)}) async-start(), calls=%async_computation.6 | async-start | bytes 294912 | tf_op jit(solution)/shard_map/reduce_scatter | solution.py:144
  756.0 135.9 %collective-permute-start.2 = (f32[1,256]{1,0:T(1,128)S(1)}, f32[1,256]{1,0:T(1,128)S(1)}, u32[]{:S(2)}, u32[]{:S(2)}) collective-permute-start(f32[1,256]{1,0:T(1,128)S(1)} %slice.80), channel_id=1, source_target_pairs={{0,8},{8,16},{16,24},{24,32},{32,40},{40,48},{48,56},{56,64},{64,7... | collective-permute-start | bytes 3080 | tf_op jit(solution)/shard_map/ppermute | solution.py:14
  898.0 130.7 %collective-permute-start.3 = (f32[1,256]{1,0:T(1,128)S(1)}, f32[1,256]{1,0:T(1,128)S(1)}, u32[]{:S(2)}, u32[]{:S(2)}) collective-permute-start(f32[1,256]{1,0:T(1,128)S(1)} %slice.83), channel_id=1, source_target_pairs={{0,504},{8,0},{16,8},{24,16},{32,24},{40,32},{48,40},{56,48},{64,5... | collective-permute-start | bytes 3080 | tf_op jit(solution)/shard_map/ppermute | solution.py:14
  1161.7 152.2 %collective-permute-start.4 = (f32[1,256]{1,0:T(1,128)S(1)}, f32[1,256]{1,0:T(1,128)S(1)}, u32[]{:S(2)}, u32[]{:S(2)}) collective-permute-start(f32[1,256]{1,0:T(1,128)S(1)} %slice.84), channel_id=1, source_target_pairs={{0,8},{8,16},{16,24},{24,32},{32,40},{40,48},{48,56},{56,64},{64,7... | collective-permute-start | bytes 3080 | tf_op jit(solution)/shard_map/ppermute | solution.py:14
  1166.6 321.5 %reduce-scatter.11.cloned.1.call-start = ((), (), s32[]{:S(2)}) async-start(), calls=%async_computation.7 | async-start | bytes 294912 | tf_op jit(solution)/shard_map/reduce_scatter | solution.py:144
  1320.0 134.3 %collective-permute-start.5 = (f32[1,256]{1,0:T(1,128)S(1)}, f32[1,256]{1,0:T(1,128)S(1)}, u32[]{:S(2)}, u32[]{:S(2)}) collective-permute-start(f32[1,256]{1,0:T(1,128)S(1)} %slice.87), channel_id=1, source_target_pairs={{0,504},{8,0},{16,8},{24,16},{32,24},{40,32},{48,40},{56,48},{64,5... | collective-permute-start | bytes 3080 | tf_op jit(solution)/shard_map/ppermute | solution.py:14
Sparse Core Ops, SparseCore 0:
  40.4 42.1 reduce-scatter.4
  743.0 39.1 reduce-scatter.6
  1166.7 41.5 reduce-scatter.8
  1453.5 34.5 reduce-scatter.10
where the time goes:
time: 1500 us
  blocking collectives  1280 us (85%)
  local copies, waits for them, and re-layouts  86.5 us (6%)
  between operations  36.6 us (2%)
  waiting for transfers between devices  33 us (2%)
  matrix products  26.5 us (2%)
  starting transfers between devices  16.8 us (1%)
  other arithmetic  16.8 us (1%)
    psum x4, blocking collectives, to_owners(): summed = lax.psum(partial_value, 'hours')  515 us
    unnamed x3, blocking collectives  367 us
    psum x3, blocking collectives, body(): dual_sum = lax.psum(dual_sq, ('hours', 'region'))  297 us
    all_gather x4, blocking collectives, body(): lax.all_gather(prices, 'region', axis=1, tiled=True)  101 us
    gather x3, local copies, waits for them, and re-layouts, body(): cap_dense = capacity_all[inverse].reshape(tech_count, node_count)  35.3 us
    gather x3, local copies, waits for them, and re-layouts, body(): jnp.sum(availability * cap_duals, axis=0).reshape(-1)[owner_cols]  35.3 us
    reduce_scatter x4, waiting for transfers between devices, body(): lax.psum_scatter(per_dest, 'region', scatter_dimension=1, tiled=True)  32.9 us
  transfers between devices with their start and end apart: 10, of which 1 were waited for; matrix products, arithmetic and copies ran while one was open for 7% of the time, Pallas kernels for 0%

commit v1 on v0

--- a/solution.py
+++ b/solution.py
@@ -161,7 +161,9 @@
                 + jnp.sum((cap_new - cap_duals) ** 2)
                 + jnp.sum((store_new - store_duals) ** 2)
             )
-            dual_sum = lax.psum(dual_sq, ("hours", "region"))
+            dual_sum = dual_sq
+            for kk in ("hours", "region"):
+                dual_sum = lax.psum(dual_sum, kk)
             weight = jnp.sqrt(weight * jnp.sqrt((dual_sum + epsilon) / (primal_sum + epsilon)))
         dispatch, capacity, inner_flow, cross_flow = (
             dispatch_new,

time: 1500 us -> 1560 us (1.040)
  blocking collectives: 1280 us -> 1320 us
    psum x3 -> x7, blocking collectives: 297 us -> 467 us  [the longest x3 296 us: body(): primal_sum = lax.psum(primal_sq, ('hours', 'region'))]
    psum x4 -> x3, blocking collectives: 515 us -> 378 us  [to_owners(): summed = lax.psum(partial_value, 'hours')]
where the time goes in v1:
time: 1560 us; the launch traced here: 1550 us
  blocking collectives  1320 us (85%)
  local copies, waits for them, and re-layouts  86.5 us (6%)
  waiting for transfers between devices  36.7 us (2%)
  between operations  36.5 us (2%)
  starting transfers between devices  26.6 us (2%)
  matrix products  26.5 us (2%)
  other arithmetic  16.8 us (1%)
    unnamed x3, blocking collectives  379 us
    psum x3, blocking collectives, to_owners(): summed = lax.psum(partial_value, 'hours')  378 us
    psum x3, blocking collectives, body(): primal_sum = lax.psum(primal_sq, ('hours', 'region'))  296 us
    psum x4, blocking collectives, body(): dual_sum = lax.psum(dual_sum, kk)  171 us
    all_gather x4, blocking collectives, body(): lax.all_gather(prices, 'region', axis=1, tiled=True)  101 us
    reduce_scatter x4, waiting for transfers between devices, body(): lax.psum_scatter(per_dest, 'region', scatter_dimension=1, tiled=True)  36.6 us
    gather x3, local copies, waits for them, and re-layouts, body(): cap_dense = capacity_all[inverse].reshape(tech_count, node_count)  35.3 us
    gather x3, local copies, waits for them, and re-layouts, body(): jnp.sum(availability * cap_duals, axis=0).reshape(-1)[owner_cols]  35.3 us
  transfers between devices with their start and end apart: 10, of which 1 were waited for; matrix products, arithmetic and copies ran while one was open for 7% of the time, Pallas kernels for 0%

profile of v1, /device:TPU:2, one launch (start us, length us, event | category | flops | bytes accessed | tf_op | source)
XLA Modules:
  0.0 1554.0 jit_solution(18008598042695098387)
XLA Ops:
  7.9 2.0 collective-permute-start
  10.0 26.6 %all_gather.21 = f32[64,1024]{1,0:T(8,128)S(1)} all-gather(f32[64,128]{1,0:T(8,128)} %param.27), channel_id=1, replica_groups=mesh['hours'=64,'region'=8] {'region'}, dimensions={1}, use_global_device_ids=true | all-gather | bytes 294912 | tf_op jit(solution)/shard_map/all_gather | solution.py:85
  39.0 1.3 fusion.74
  41.2 11.8 gather_fusion
  53.0 126.8 %psum.91 = f32[2048]{0:T(1024)S(1)} all-reduce(f32[2048]{0:T(1024)S(1)} %gather_fusion), channel_id=1, replica_groups=mesh['hours'=64,'region'=8] {'hours'}, use_global_device_ids=true, to_apply=%region_5.6 | all-reduce | flops 2048 | bytes 16384 | tf_op jit(solution)/shard_map/psum | solution.py:22
  179.7 1.3 dynamic-slice
  182.5 126.4 %all-reduce = f32[2048]{0:T(1024)S(1)} all-reduce(f32[2048]{0:T(1024)S(1)} %multiply_dynamic-update-slice_fusion), channel_id=1, replica_groups=mesh['hours'=64,'region'=8] {'hours'}, use_global_device_ids=true, to_apply=%add | all-reduce | flops 2048 | bytes 16384
  308.9 5.0 sort.17
  314.0 11.8 gather_fusion.1
  325.8 1.1 multiply_reduce_fusion.6
  328.8 11.8 gather_fusion.2
  346.0 6.6 collective-permute-start.1
  352.6 95.6 %psum.94 = f32[]{:T(128)} all-reduce(f32[]{:T(128)S(6)} %add.321), channel_id=1, replica_groups=mesh['hours'=64,'region'=8] {'hours','region'}, use_global_device_ids=true, to_apply=%region_17.18 | all-reduce | flops 1 | bytes 8 | tf_op jit(solution)/shard_map/psum | solution.py:130
  448.9 1.0 fusion.67
  452.7 126.3 %all-reduce.5 = (f32[2048]{0:T(1024)S(1)}, f32[]{:T(128)}) all-reduce(f32[2048]{0:T(1024)S(1)} %gather_fusion.2, f32[]{:T(128)S(6)} %add.315), channel_id=1, replica_groups=mesh['hours'=64,'region'=8] {'hours'}, use_global_device_ids=true, to_apply=%region_22.23 | all-reduce | flops 2049 | bytes 16392 | tf_op jit(solution)/shard_map/psum | solution.py:22
  579.0 14.8 psum.93
  594.6 24.8 %all_gather.23 = f32[64,1024]{1,0:T(8,128)S(1)} all-gather(f32[64,128]{1,0:T(8,128)S(1)} %get-tuple-element.56), channel_id=1, replica_groups=mesh['hours'=64,'region'=8] {'region'}, dimensions={1}, use_global_device_ids=true | all-gather | bytes 294912 | tf_op jit(solution)/shard_map/all_gather | solution.py:85
  619.5 1.0 multiply_reduce_fusion.17
  621.3 126.1 %all-reduce.1 = f32[2048]{0:T(1024)S(1)} all-reduce(f32[2048]{0:T(1024)S(1)} %subtract_dynamic-update-slice_fusion.1), channel_id=1, replica_groups=mesh['hours'=64,'region'=8] {'hours'}, use_global_device_ids=true, to_apply=%add.1 | all-reduce | flops 2048 | bytes 16384
  747.4 11.8 gather_fusion.3
  760.6 1.9 collective-permute-start.2
  764.1 1.3 fusion.72
  765.5 1.2 multiply_reduce_fusion.3
  767.0 11.8 gather_fusion.4
  781.4 1.0 multiply_reduce_fusion.15
  783.6 7.0 collective-permute-start.3
  790.6 100.1 %psum.98 = f32[]{:T(128)} all-reduce(f32[]{:T(128)S(6)} %add.341), channel_id=1, replica_groups=mesh['hours'=64,'region'=8] {'hours','region'}, use_global_device_ids=true, to_apply=%region_33.34 | all-reduce | flops 1 | bytes 8 | tf_op jit(solution)/shard_map/psum | solution.py:130
  891.4 1.0 fusion.63
  895.2 124.9 %all-reduce.4 = (f32[2048]{0:T(1024)S(1)}, f32[]{:T(128)}) all-reduce(f32[2048]{0:T(1024)S(1)} %gather_fusion.4, f32[]{:T(128)S(6)} %add.335), channel_id=1, replica_groups=mesh['hours'=64,'region'=8] {'hours'}, use_global_device_ids=true, to_apply=%region_38.39 | all-reduce | flops 2049 | bytes 16392 | tf_op jit(solution)/shard_map/psum | solution.py:22
  1020.1 15.9 %psum.97 = f32[]{:T(128)} all-reduce(f32[]{:T(128)} %get-tuple-element.25), channel_id=1, replica_groups=mesh['hours'=64,'region'=8] {'region'}, use_global_device_ids=true, to_apply=%region_26.27 | all-reduce | flops 1 | bytes 8 | tf_op jit(solution)/shard_map/psum | solution.py:166
  1037.5 1.0 multiply_reduce_fusion.12
  1038.6 24.8 %all_gather.25 = f32[64,1024]{1,0:T(8,128)S(1)} all-gather(f32[64,128]{1,0:T(8,128)S(1)} %get-tuple-element.63), channel_id=1, replica_groups=mesh['hours'=64,'region'=8] {'region'}, dimensions={1}, use_global_device_ids=true | all-gather | bytes 294912 | tf_op jit(solution)/shard_map/all_gather | solution.py:85
  1064.1 126.1 %all-reduce.2 = f32[2048]{0:T(1024)S(1)} all-reduce(f32[2048]{0:T(1024)S(1)} %subtract_dynamic-update-slice_fusion), channel_id=1, replica_groups=mesh['hours'=64,'region'=8] {'hours'}, use_global_device_ids=true, to_apply=%add.2 | all-reduce | flops 2048 | bytes 16384
  1190.3 11.8 gather_fusion.5
  1202.1 1.9 collective-permute-start.4
  1205.6 1.3 fusion.70
  1207.0 1.4 multiply_reduce_fusion
  1208.8 11.8 gather_fusion.6
  1225.3 7.0 collective-permute-start.5
  1232.3 100.0 %psum.102 = f32[]{:T(128)} all-reduce(f32[]{:T(128)S(6)} %add.361), channel_id=1, replica_groups=mesh['hours'=64,'region'=8] {'hours','region'}, use_global_device_ids=true, to_apply=%region_49.50 | all-reduce | flops 1 | bytes 8 | tf_op jit(solution)/shard_map/psum | solution.py:130
  1332.3 1.0 fusion.59
  1336.7 124.9 %all-reduce.3 = (f32[]{:T(128)}, f32[2048]{0:T(1024)S(1)}) all-reduce(f32[]{:T(128)S(6)} %add.355, f32[2048]{0:T(1024)S(1)} %gather_fusion.6), channel_id=1, replica_groups=mesh['hours'=64,'region'=8] {'hours'}, use_global_device_ids=true, to_apply=%region_41.42 | all-reduce | flops 2049 | bytes 16392 | tf_op jit(solution)/shard_map/psum | solution.py:166
  1461.6 15.7 %psum.101 = f32[]{:T(128)} all-reduce(f32[]{:T(128)} %get-tuple-element.22), channel_id=1, replica_groups=mesh['hours'=64,'region'=8] {'region'}, use_global_device_ids=true, to_apply=%region_42.43 | all-reduce | flops 1 | bytes 8 | tf_op jit(solution)/shard_map/psum | solution.py:166
  1478.1 24.8 %all_gather.27 = f32[64,1024]{1,0:T(8,128)S(1)} all-gather(f32[64,128]{1,0:T(8,128)S(1)} %get-tuple-element.70), channel_id=1, replica_groups=mesh['hours'=64,'region'=8] {'region'}, dimensions={1}, use_global_device_ids=true | all-gather | bytes 294912 | tf_op jit(solution)/shard_map/all_gather | solution.py:85
  1503.3 1.6 subtract_reduce_fusion
  1505.9 1.3 fusion.68
  1509.1 36.6 %reduce-scatter.11.cloned.1.call-done = f32[64,128]{1,0:T(8,128)} async-done(((f32[64,1024]{1,0:T(8,128)}), f32[64,128]{1,0:T(8,128)}) %reduce-scatter.11.cloned.1.call-update) | async-done | bytes 32784 | tf_op jit(solution)/shard_map/reduce_scatter | solution.py:144
  1545.6 1.0 fusion.55
  (105 shorter events, 23.8 us)
Async XLA Ops:
  7.2 441.7 %reduce-scatter.5.cloned.1.call-start = ((), (), s32[]{:S(2)}) async-start(), calls=%async_computation.4 | async-start | bytes 294912 | tf_op jit(solution)/shard_map/reduce_scatter | solution.py:144
  7.9 2.1 copy-start.9
  7.9 335.2 %collective-permute-start = (f32[1,256]{1,0:T(1,128)S(1)}, f32[1,256]{1,0:T(1,128)S(1)}, u32[]{:S(2)}, u32[]{:S(2)}) collective-permute-start(f32[1,256]{1,0:T(1,128)S(1)} %bitcast.122), channel_id=1, source_target_pairs={{0,8},{8,16},{16,24},{24,32},{32,40},{40,48},{48,56},{56,64},{64,7... | collective-permute-start | bytes 3080 | tf_op jit(solution)/shard_map/ppermute | solution.py:14
  36.6 0.7 copy-start.13
  36.6 0.7 copy-start.12
  37.2 0.8 copy-start.1
  37.3 3.8 copy-start
  40.3 851.1 %reduce-scatter.7.cloned.1.call-start = ((), (), s32[]{:S(2)}) async-start(), calls=%async_computation.5 | async-start | bytes 294912 | tf_op jit(solution)/shard_map/reduce_scatter | solution.py:144
  40.3 0.7 copy-start.11
  40.3 0.7 copy-start.5
  40.4 0.7 copy-start.10
  181.0 0.7 copy-start.8
  314.0 11.8 copy-start.3
  328.1 0.7 copy-start.7
  343.1 0.7 copy-start.4
  346.0 413.2 %collective-permute-start.1 = (f32[1,256]{1,0:T(1,128)S(1)}, f32[1,256]{1,0:T(1,128)S(1)}, u32[]{:S(2)}, u32[]{:S(2)}) collective-permute-start(f32[1,256]{1,0:T(1,128)S(1)} %slice.79), channel_id=1, source_target_pairs={{0,504},{8,0},{16,8},{24,16},{32,24},{40,32},{48,40},{56,48},{64,5... | collective-permute-start | bytes 3080 | tf_op jit(solution)/shard_map/ppermute | solution.py:14
  448.9 1.1 copy-start.2
  759.2 0.7 copy-start.6
  760.6 20.8 %collective-permute-start.2 = (f32[1,256]{1,0:T(1,128)S(1)}, f32[1,256]{1,0:T(1,128)S(1)}, u32[]{:S(2)}, u32[]{:S(2)}) collective-permute-start(f32[1,256]{1,0:T(1,128)S(1)} %slice.80), channel_id=1, source_target_pairs={{0,8},{8,16},{16,24},{24,32},{32,40},{40,48},{48,56},{56,64},{64,7... | collective-permute-start | bytes 3080 | tf_op jit(solution)/shard_map/ppermute | solution.py:14
  765.4 566.8 %reduce-scatter.9.cloned.1.call-start = ((), (), s32[]{:S(2)}) async-start(), calls=%async_computation.6 | async-start | bytes 294912 | tf_op jit(solution)/shard_map/reduce_scatter | solution.py:144
  783.6 279.7 %collective-permute-start.3 = (f32[1,256]{1,0:T(1,128)S(1)}, f32[1,256]{1,0:T(1,128)S(1)}, u32[]{:S(2)}, u32[]{:S(2)}) collective-permute-start(f32[1,256]{1,0:T(1,128)S(1)} %slice.83), channel_id=1, source_target_pairs={{0,504},{8,0},{16,8},{24,16},{32,24},{40,32},{48,40},{56,48},{64,5... | collective-permute-start | bytes 3080 | tf_op jit(solution)/shard_map/ppermute | solution.py:14
  1202.1 21.0 %collective-permute-start.4 = (f32[1,256]{1,0:T(1,128)S(1)}, f32[1,256]{1,0:T(1,128)S(1)}, u32[]{:S(2)}, u32[]{:S(2)}) collective-permute-start(f32[1,256]{1,0:T(1,128)S(1)} %slice.84), channel_id=1, source_target_pairs={{0,8},{8,16},{16,24},{24,32},{32,40},{40,48},{48,56},{56,64},{64,7... | collective-permute-start | bytes 3080 | tf_op jit(solution)/shard_map/ppermute | solution.py:14
  1207.0 338.7 %reduce-scatter.11.cloned.1.call-start = ((), (), s32[]{:S(2)}) async-start(), calls=%async_computation.7 | async-start | bytes 294912 | tf_op jit(solution)/shard_map/reduce_scatter | solution.py:144
  1225.3 282.8 %collective-permute-start.5 = (f32[1,256]{1,0:T(1,128)S(1)}, f32[1,256]{1,0:T(1,128)S(1)}, u32[]{:S(2)}, u32[]{:S(2)}) collective-permute-start(f32[1,256]{1,0:T(1,128)S(1)} %slice.87), channel_id=1, source_target_pairs={{0,504},{8,0},{16,8},{24,16},{32,24},{40,32},{48,40},{56,48},{64,5... | collective-permute-start | bytes 3080 | tf_op jit(solution)/shard_map/ppermute | solution.py:14
Sparse Core Ops, SparseCore 0:
  40.4 42.1 reduce-scatter.4
  765.6 40.8 reduce-scatter.6
  1207.1 40.5 reduce-scatter.8
  1507.3 38.2 reduce-scatter.10
